TPU v7x, 32 devices: a whole 2x2x4 slice. The times are simulated.
32 devices in a mesh: seg: 8 (over y, x, core), row: 4 (over z).
Axes of the slice: x: 2, y: 2, z: 4, core: 2. Of those that a mesh axis runs over, the one named last changes fastest.
Arguments:
- left_env: bfloat16 [8, 512, 12, 512], P('seg', 'row'), may hold values from -4 to 4, as said below
- right_env: bfloat16 [8, 512, 12, 512], P('seg'), may hold values from -4 to 4, as said below
- site_operator: bfloat16 [4, 12, 12, 4], replicated, may hold values from -1 to 2, as said below
- start_vector: float32 [8, 512, 4, 512], P('seg', 'row'), may hold values from -6 to 6
Outputs:
- last_vector: float32 [8, 512, 4, 512], P('seg', 'row')
- alpha_values: float32 [8, 2], P('seg')
- beta_values: float32 [8, 2], P('seg')
Inputs may be any that keep to these rules, and one draw needn't show every extreme that they name: left_env[i, a, w, c] = left_env[i, c, w, a]. right_env[i, a, w, c] = right_env[i, c, w, a]. site_operator[s, v, w, r] = site_operator[r, v, w, s].
All inputs are finite; a program needn't handle non-finite values.
Results may differ from a plain program's by a relative error of at most 0.0076.
Values may be sent and summed in bfloat16 or wider, within the bound.
A program may use at most 128 MiB of HBM per device.

v0:
```python
import jax
import jax.numpy as jnp
from jax import lax
from jax.sharding import PartitionSpec as P

ITERS = 2


def passed_along(value, axis, steps):
    count = lax.axis_size(axis)
    initial, last = (max(0, -steps), min(count, count - steps))
    return lax.ppermute(value, axis, [(source, source + steps) for source in range(initial, last)])


def local(left_env, right_env, site_operator, start_vector):
    rows_here = left_env.shape[1]
    channels = left_env.shape[2]
    bond_width = left_env.shape[3]
    physical = site_operator.shape[0]
    entries = float(bond_width * physical * bond_width)
    left_local = left_env[0]
    operator_mat = site_operator.reshape(physical * channels, channels * physical)
    last_segment = lax.axis_index("seg") == lax.axis_size("seg") - 1
    received = passed_along(right_env, "seg", -1)
    right_used = jnp.where(last_segment, right_env, received)
    right_mat = right_used[0].reshape(bond_width, channels * bond_width)
    start_local = start_vector[0]
    norm_start = lax.psum(jnp.sum(start_local * start_local), "row") / entries
    current = start_local / jnp.sqrt(norm_start + 1e-06)
    previous = jnp.zeros_like(current)
    beta_prev = jnp.zeros((), jnp.float32)
    alpha_list = []
    beta_list = []
    for step_index in range(ITERS):
        lowered = current.astype(jnp.bfloat16)
        gathered = lax.all_gather(lowered, "row", axis=0, tiled=True)
        contracted = jnp.dot(
            left_local.reshape(rows_here * channels, bond_width),
            gathered.reshape(bond_width, physical * bond_width),
            preferred_element_type=jnp.float32,
        )
        contracted = contracted.astype(jnp.bfloat16).reshape(
            rows_here, channels * physical, bond_width
        )
        mixed = jnp.einsum(
            "ik,akb->aib", operator_mat, contracted, preferred_element_type=jnp.float32
        )
        mixed = mixed.astype(jnp.bfloat16).reshape(rows_here, physical, channels * bond_width)
        image = jnp.einsum("asc,bc->asb", mixed, right_mat, preferred_element_type=jnp.float32)
        image_image, image_curr, image_prev, curr_curr, prev_prev, curr_prev = lax.psum(
            (
                jnp.sum(image * image),
                jnp.sum(image * current),
                jnp.sum(image * previous),
                jnp.sum(current * current),
                jnp.sum(previous * previous),
                jnp.sum(current * previous),
            ),
            "row",
        )
        alpha = image_curr / entries
        norm_sq = (
            image_image
            - 2.0 * alpha * image_curr
            - 2.0 * beta_prev * image_prev
            + alpha * alpha * curr_curr
            + beta_prev * beta_prev * prev_prev
            + 2.0 * alpha * beta_prev * curr_prev
        ) / entries
        residual_vec = image - alpha * current - beta_prev * previous
        beta_next = jnp.sqrt(norm_sq + 1e-06)
        previous = current
        current = residual_vec / beta_next
        beta_prev = beta_next
        alpha_list.append(alpha)
        beta_list.append(beta_next)
    alpha_values = jnp.stack(alpha_list).reshape(1, ITERS)
    beta_values = jnp.stack(beta_list).reshape(1, ITERS)
    return (current[None], alpha_values, beta_values)


def solution(mesh):
    placed = (
        P("seg", "row", None, None),
        P("seg", None, None, None),
        P(),
        P("seg", "row", None, None),
    )
    return jax.shard_map(
        local,
        mesh=mesh,
        in_specs=placed,
        out_specs=(P("seg", "row", None, None), P("seg", None), P("seg", None)),
        check_vma=False,
    )
```

profile of v0, /device:TPU:0, one launch (start us, length us, event | category | flops | bytes accessed | tf_op | source)
XLA Modules:
  0.0 300.8 jit_solution(16806568525329012419)
XLA Ops:
  7.2 0.0 copy-start
  7.2 0.0 all-gather.3.cloned.1.call-start
  7.2 8.7 %copy.18 = bf16[1,512,12,512]{1,3,2,0:T(8,128)(2,1)} copy(bf16[1,512,12,512]{3,1,2,0:T(8,128)(2,1)} %param.5) | data formatting | bytes 12582912 | tf_op args[1]
  15.9 0.0 copy-start.1
  15.9 1.4 collective-permute-start
  17.4 0.0 copy-done
  17.4 1.1 multiply_reduce_fusion.5
  18.5 14.0 %psum.87 = f32[]{:T(128)} all-reduce(f32[]{:T(128)} %multiply_reduce_fusion.5), channel_id=1, replica_groups=mesh['seg'=8,'row'=4] {'row'}, use_global_device_ids=true, to_apply=%region_1.2 | all-reduce | flops 1 | bytes 8 | tf_op jit(solution)/shard_map/psum | solution.py:28
  33.2 1.1 bitcast_convert_fusion
  34.3 0.0 all-gather.3.cloned.1.call-update
  34.3 0.0 all-gather.5.cloned.1.call-start
  34.4 2.3 copy.13
  36.7 1.4 reshape_squeeze.7
  38.1 0.0 copy-done.1
  38.1 0.2 copy.15
  38.3 0.1 reshape.38
  38.4 41.6 %all-gather.3.cloned.1.call-done = bf16[512,4,512]{2,0,1:T(8,128)(2,1)} async-done(((bf16[128,4,512]{2,0,1:T(8,128)(2,1)}), bf16[512,4,512]{2,0,1:T(8,128)(2,1)}) %all-gather.3.cloned.1.call-update) | async-done | bytes 2097168 | tf_op jit(solution)/shard_map/all_gather | solution.py:36
  80.0 2.8 copy.12
  82.8 6.8 %fusion = bf16[1536,2048]{0,1:T(8,128)(2,1)} fusion(bf16[512,2048]{0,1:T(8,128)(2,1)S(1)} %bitcast.73, bf16[1536,512]{1,0:T(8,128)(2,1)} %reshape_squeeze.7), kind=kOutput, calls=%fused_computation.2 | convolution fusion | flops 3224371200 | bytes 9961472 | tf_op jit(solution)/shard_map/dot_general | solution.py:37
  89.6 8.6 %copy.14 = bf16[1536,2048]{1,0:T(8,128)(2,1)} copy(bf16[1536,2048]{0,1:T(8,128)(2,1)} %fusion) | data formatting | bytes 12582912 | tf_op jit(solution)/shard_map/convert_element_type | solution.py:42
  98.2 10.7 %reshape.37 = bf16[128,48,512]{2,1,0:T(8,128)(2,1)} reshape(bf16[1536,2048]{1,0:T(8,128)(2,1)} %copy.14) | data formatting | bytes 12582912 | tf_op jit(solution)/shard_map/reshape | solution.py:42
  108.9 7.3 %convert_bitcast_fusion.1 = bf16[128,48,512]{2,1,0:T(8,128)(2,1)} fusion(bf16[128,48,512]{2,1,0:T(8,128)(2,1)} %reshape.37, bf16[48,48]{0,1:T(8,128)(2,1)S(1)} %reshape.38), kind=kOutput, calls=%fused_computation.9 | convolution fusion | flops 305135616 | bytes 12587520 | tf_op jit(solution)/shard_map/ik,akb->aib/dot_general | solution.py:45
  116.2 13.6 %reshape.39 = bf16[128,4,6144]{2,1,0:T(4,128)(2,1)} reshape(bf16[128,48,512]{2,1,0:T(8,128)(2,1)} %convert_bitcast_fusion.1) | data formatting | bytes 12582912 | tf_op jit(solution)/shard_map/reshape | solution.py:48
  129.8 0.0 collective-permute-done
  129.8 6.1 %broadcast_select_fusion = bf16[1,512,12,512]{1,3,2,0:T(8,128)(2,1)} fusion(bf16[1,512,12,512]{1,3,2,0:T(8,128)(2,1)} %copy.18, bf16[1,512,12,512]{1,3,2,0:T(8,128)(2,1)} %collective-permute-done, pred[]{:T(512)S(6)} %eq.3), kind=kLoop, calls=%fused_computation.10 | loop fusion | flops 3145728 | bytes 18874368 | tf_op jit(solution)/shard_map/jit(_where)/select_n | solution.py:25
  135.9 11.5 %fusion.10 = (f32[]{:T(128)}, f32[]{:T(128)}, f32[]{:T(128)}, f32[]{:T(128)}, f32[]{:T(128)}, /*index=5*/f32[128,4,512]{2,0,1:T(8,128)S(1)}) fusion(f32[]{:T(128)S(6)} %sqrt.9, f32[1,128,4,512]{3,2,1,0:T(4,128)S(1)} %copy-done, bf16[512,6144,1]{0,1,2:T(8,128)(2,1)} %bitcast.70, bf16[128,4,6144]{2,1,0:T(4,128)(2,1)} %reshape.39), kind=kOutput, calls=%fused_computation.23 | convolution fusion | flops 3224109056 | bytes 14680088 | tf_op jit(solution)/shard_map/asc,bc->asb/dot_general | solution.py:49
  147.4 10.9 %all-reduce.1 = (f32[]{:T(128)}, f32[]{:T(128)}, f32[]{:T(128)}, f32[]{:T(128)}, f32[]{:T(128)}, /*index=5*/f32[]{:T(128)}) all-reduce(f32[]{:T(128)} %get-tuple-element.18, f32[]{:T(128)} %get-tuple-element.16, f32[]{:T(128)} %get-tuple-element.17, f32[]{:T(128)} %get-tuple-element.15, ...), channel_id=1, replica_groups=mesh['seg'=8,'row'=4] {'row'}, use_global_device_ids=true, to_apply=%region_5.6 | all-reduce | flops 6 | bytes 48 | tf_op jit(solution)/shard_map/psum | solution.py:50
  165.4 1.2 fusion.18
  166.6 0.0 all-gather.5.cloned.1.call-update
  167.3 43.9 %all-gather.5.cloned.1.call-done = bf16[512,4,512]{2,0,1:T(8,128)(2,1)} async-done(((bf16[128,4,512]{2,0,1:T(8,128)(2,1)}), bf16[512,4,512]{2,0,1:T(8,128)(2,1)}) %all-gather.5.cloned.1.call-update) | async-done | bytes 2097168 | tf_op jit(solution)/shard_map/all_gather | solution.py:36
  211.2 4.2 %copy.21 = bf16[512,4,512]{0,2,1:T(8,128)(2,1)} copy(bf16[512,4,512]{2,0,1:T(8,128)(2,1)} %all-gather.5.cloned.1.call-done) | data formatting | bytes 4194304 | tf_op jit(solution)/shard_map/all_gather | solution.py:36
  215.3 8.2 %fusion.1 = bf16[1536,2048]{0,1:T(8,128)(2,1)} fusion(bf16[512,2048]{0,1:T(8,128)(2,1)} %bitcast.72, bf16[1536,512]{1,0:T(8,128)(2,1)} %reshape_squeeze.7), kind=kOutput, calls=%fused_computation.3 | convolution fusion | flops 3224371200 | bytes 9961472 | tf_op jit(solution)/shard_map/dot_general | solution.py:37
  223.5 8.6 %copy.22 = bf16[1536,2048]{1,0:T(8,128)(2,1)} copy(bf16[1536,2048]{0,1:T(8,128)(2,1)} %fusion.1) | data formatting | bytes 12582912 | tf_op jit(solution)/shard_map/convert_element_type | solution.py:42
  232.1 10.7 %reshape.41 = bf16[128,48,512]{2,1,0:T(8,128)(2,1)} reshape(bf16[1536,2048]{1,0:T(8,128)(2,1)} %copy.22) | data formatting | bytes 12582912 | tf_op jit(solution)/shard_map/reshape | solution.py:42
  242.8 7.2 %convert_bitcast_fusion = bf16[128,48,512]{2,1,0:T(8,128)(2,1)} fusion(bf16[128,48,512]{2,1,0:T(8,128)(2,1)} %reshape.41, bf16[48,48]{0,1:T(8,128)(2,1)S(1)} %reshape.38), kind=kOutput, calls=%fused_computation.8 | convolution fusion | flops 305135616 | bytes 12587520 | tf_op jit(solution)/shard_map/ik,akb->aib/dot_general | solution.py:45
  250.0 13.6 %reshape.42 = bf16[128,4,6144]{2,1,0:T(4,128)(2,1)} reshape(bf16[128,48,512]{2,1,0:T(8,128)(2,1)} %convert_bitcast_fusion) | data formatting | bytes 12582912 | tf_op jit(solution)/shard_map/reshape | solution.py:48
  263.6 11.5 %fusion.15 = (f32[]{:T(128)}, f32[]{:T(128)}, f32[]{:T(128)}, f32[]{:T(128)}, f32[]{:T(128)}, /*index=5*/f32[128,4,512]{2,0,1:T(8,128)S(1)}) fusion(f32[128,4,512]{2,0,1:T(8,128)S(1)} %get-tuple-element.31, f32[]{:T(128)S(6)} %sqrt.9, f32[1,128,4,512]{3,2,1,0:T(4,128)S(1)} %copy-done, bf16[512,6144,1]{0,1,2:T(8,128)(2,1)} %bitcast.71, ...), kind=kOutput, calls=%fused_computation.28 | convolution fusion | flops 3224109056 | bytes 15728664 | tf_op jit(solution)/shard_map/asc,bc->asb/dot_general | solution.py:49
  275.1 10.2 %all-reduce = (f32[]{:T(128)}, f32[]{:T(128)}, f32[]{:T(128)}, f32[]{:T(128)}, f32[]{:T(128)}) all-reduce(f32[]{:T(128)} %get-tuple-element.12, f32[]{:T(128)} %get-tuple-element.11, f32[]{:T(128)} %get-tuple-element.10, f32[]{:T(128)} %get-tuple-element.13, f32[]{:T(128)} %get-tuple-element.9), channel_id=1, replica_groups=mesh['seg'=8,'row'=4] {'row'}, use_global_device_ids=true, to_apply=%region_16.17 | all-reduce | flops 5 | bytes 40 | tf_op jit(solution)/shard_map/psum | solution.py:50
  291.2 0.5 fusion.13
  291.7 1.6 copy.26
  293.3 0.6 maximum_bitcast_fusion
Async XLA Ops:
  7.2 10.2 %copy-start = (f32[1,128,4,512]{3,2,1,0:T(4,128)S(1)}, f32[1,128,4,512]{3,2,1,0:T(4,128)}, u32[]{:S(2)}) copy-start(f32[1,128,4,512]{3,2,1,0:T(4,128)} %param.7) | copy-start | bytes 3145732
  7.2 72.9 %all-gather.3.cloned.1.call-start = ((), (), s32[]{:S(2)}) async-start(), calls=%async_computation | async-start | bytes 2621440 | tf_op jit(solution)/shard_map/all_gather | solution.py:36
  15.9 22.1 %copy-start.1 = (bf16[4,12,12,4]{2,3,1,0:T(4,128)(2,1)S(1)}, bf16[4,12,12,4]{2,3,1,0:T(4,128)(2,1)}, u32[]{:S(2)}) copy-start(bf16[4,12,12,4]{2,3,1,0:T(4,128)(2,1)} %param.6) | copy-start | bytes 13828
  15.9 113.9 %collective-permute-start = (bf16[1,512,12,512]{1,3,2,0:T(8,128)(2,1)}, bf16[1,512,12,512]{1,3,2,0:T(8,128)(2,1)}, u32[]{:S(2)}, u32[]{:S(2)}) collective-permute-start(bf16[1,512,12,512]{1,3,2,0:T(8,128)(2,1)} %copy.18), channel_id=1, source_target_pairs={{4,0},{8,4},{12,8},{16,12},{20,16},{24,20},{28,24},{5,1},{9,5},{13... | collective-permute-start | bytes 18874376 | tf_op jit(solution)/shard_map/ppermute | solution.py:12
  34.3 176.8 %all-gather.5.cloned.1.call-start = ((), (), s32[]{:S(2)}) async-start(), calls=%async_computation.1 | async-start | bytes 2621440 | tf_op jit(solution)/shard_map/all_gather | solution.py:36
Sparse Core Ops, SparseCore 0:
  34.4 45.5 all-gather.2
  166.7 44.3 all-gather.4
where the time goes:
time: 303 us; the launch traced here: 301 us
  local copies, waits for them, and re-layouts  87.1 us (29%)
  waiting for transfers between devices  85.5 us (28%)
  matrix products  52.4 us (17%)
  blocking collectives  35.1 us (12%)
  between operations  28.4 us (9%)
  other arithmetic  10.6 us (3%)
    all_gather x2, waiting for transfers between devices, local(): gathered = lax.all_gather(lowered, 'row', axis=0, tiled=True)  85.5 us
    reshape x2, local copies, waits for them, and re-layouts, local(): mixed.astype(jnp.bfloat16)  27.2 us
    dot_general x2, matrix products, local(): jnp.einsum('asc,bc->asb', mixed, right_mat, preferred_element_type=jnp.fl...  22.9 us
    reshape x2, local copies, waits for them, and re-layouts, local(): contracted.astype(jnp.bfloat16)  21.4 us
    psum x2, blocking collectives, local(): lax.psum((jnp.sum(image * image), jnp.sum(image * current), jnp.sum(image...  21.1 us
    convert_element_type x2, local copies, waits for them, and re-layouts, local(): contracted.astype(jnp.bfloat16)  17.2 us
    dot_general x2, matrix products, local(): jnp.dot(left_local.reshape(rows_here * channels, bond_width), gathered.re...  14.9 us
    dot_general x2, matrix products, local(): jnp.einsum('ik,akb->aib', operator_mat, contracted, preferred_element_typ...  14.6 us
  transfers between devices with their start and end apart: 3, of which 2 were waited for; matrix products, arithmetic and copies ran while one was open for 19% of the time, Pallas kernels for 0%

commit v1 on v0

--- a/solution.py
+++ b/solution.py
@@ -1,9 +1,27 @@
+import functools
 import jax
 import jax.numpy as jnp
 from jax import lax
 from jax.sharding import PartitionSpec as P
 
 ITERS = 2
+
+
+def drive_the_meshes(local_values, axis_id, which_dim):
+    in_order = [local_values]
+    k_all = jax.lax.psum(1, axis_id)
+    for dd in range(k_all - 1):
+        f_now = jax.lax.ppermute(
+            in_order[-1], axis_id, [(c, (c + 1) % k_all) for c in range(k_all)]
+        )
+        in_order.append(f_now)
+    extra = jnp.concatenate(in_order[::-1], axis=which_dim)
+    return jnp.roll(
+        extra, (jax.lax.axis_index(axis_id) + 1) * local_values.shape[which_dim], axis=which_dim
+    )
+
+
+lift_shifts_all = functools.partial(drive_the_meshes, axis_id="row", which_dim=0)
 
 
 def passed_along(value, axis, steps):
@@ -33,7 +51,7 @@
     beta_list = []
     for step_index in range(ITERS):
         lowered = current.astype(jnp.bfloat16)
-        gathered = lax.all_gather(lowered, "row", axis=0, tiled=True)
+        gathered = lift_shifts_all(lowered)
         contracted = jnp.dot(
             left_local.reshape(rows_here * channels, bond_width),
             gathered.reshape(bond_width, physical * bond_width),

time: 303 us -> 290 us (0.957)
  waiting for transfers between devices: 85.5 us -> 69.6 us
  between operations: 28.4 us -> 15.1 us
  other arithmetic: 10.6 us -> 19.1 us
  starting transfers between devices: 1.49 us -> 6.5 us
    all_gather x2 -> x0, waiting for transfers between devices: 85.5 us -> none  [local(): gathered = lax.all_gather(lowered, 'row', axis=0, tiled=True)]
    ppermute x0 -> x6, waiting for transfers between devices: none -> 69.6 us  [drive_the_meshes(): jax.lax.ppermute(in_order[-1], axis_id, [(c, (c + 1) % k_all) for c in ra...]
    concatenate x0 -> x2, other arithmetic: none -> 9.15 us  [drive_the_meshes(): jnp.roll(extra, (jax.lax.axis_index(axis_id) + 1) * local_values.shape[wh...]
    all_gather x2 -> x0, local copies, waits for them, and re-layouts: 6.95 us -> none  [local(): gathered = lax.all_gather(lowered, 'row', axis=0, tiled=True)]
    ppermute x0 -> x6, starting transfers between devices: none -> 5.22 us  [drive_the_meshes(): jax.lax.ppermute(in_order[-1], axis_id, [(c, (c + 1) % k_all) for c in ra...]
    dynamic_slice x0 -> x2, local copies, waits for them, and re-layouts: none -> 4.82 us  [drive_the_meshes(): jnp.roll(extra, (jax.lax.axis_index(axis_id) + 1) * local_values.shape[wh...]
    unnamed x8 -> x20, local copies, waits for them, and re-layouts: 12.9 us -> 16.1 us
  transfers between devices with their start and end apart: 3 -> 7, of which waited for: 2 -> 6; matrix products, arithmetic and copies ran while one was open for 19% -> 21% of each run, Pallas kernels for 0% -> 0%
where the time goes in v1:
time: 290 us; the launch traced here: 286 us
  local copies, waits for them, and re-layouts  88.5 us (31%)
  waiting for transfers between devices  69.6 us (24%)
  matrix products  53.9 us (19%)
  blocking collectives  33.5 us (12%)
  other arithmetic  19.1 us (7%)
  between operations  15.1 us (5%)
  starting transfers between devices  6.5 us (2%)
    ppermute x6, waiting for transfers between devices, drive_the_meshes(): jax.lax.ppermute(in_order[-1], axis_id, [(c, (c + 1) % k_all) for c in ra...  69.6 us
    reshape x2, local copies, waits for them, and re-layouts, local(): mixed.astype(jnp.bfloat16)  27.2 us
    dot_general x2, matrix products, local(): jnp.einsum('asc,bc->asb', mixed, right_mat, preferred_element_type=jnp.fl...  23.2 us
    reshape x2, local copies, waits for them, and re-layouts, local(): contracted.astype(jnp.bfloat16)  21.5 us
    psum x2, blocking collectives, local(): lax.psum((jnp.sum(image * image), jnp.sum(image * current), jnp.sum(image...  19.4 us
    convert_element_type x2, local copies, waits for them, and re-layouts, local(): contracted.astype(jnp.bfloat16)  17.3 us
    dot_general x2, matrix products, local(): jnp.dot(left_local.reshape(rows_here * channels, bond_width), gathered.re...  16.3 us
    unnamed x20, local copies, waits for them, and re-layouts  16.1 us
  transfers between devices with their start and end apart: 7, of which 6 were waited for; matrix products, arithmetic and copies ran while one was open for 21% of the time, Pallas kernels for 0%

profile of v1, /device:TPU:0, one launch (start us, length us, event | category | flops | bytes accessed | tf_op | source)
XLA Modules:
  0.0 286.1 jit_solution(4656570897740891925)
XLA Ops:
  0.6 0.0 copy-start
  0.6 8.7 %copy.18 = bf16[1,512,12,512]{1,3,2,0:T(8,128)(2,1)} copy(bf16[1,512,12,512]{3,1,2,0:T(8,128)(2,1)} %param.7) | data formatting | bytes 12582912 | tf_op args[1]
  9.4 1.3 collective-permute-start.3
  10.6 0.0 copy-done
  10.7 1.1 multiply_reduce_fusion.5
  11.8 14.0 %psum.87 = f32[]{:T(128)} all-reduce(f32[]{:T(128)} %multiply_reduce_fusion.5), channel_id=1, replica_groups=mesh['seg'=8,'row'=4] {'row'}, use_global_device_ids=true, to_apply=%region_1.2 | all-reduce | flops 1 | bytes 8 | tf_op jit(solution)/shard_map/psum | solution.py:46
  26.5 0.0 copy-start.7
  26.5 0.3 bitcast_convert_fusion
  26.8 0.0 copy-start.2
  26.8 0.8 copy-done.2
  27.6 0.0 collective-permute-start
  27.6 14.9 %collective-permute-done = bf16[128,4,512]{2,0,1:T(8,128)(2,1)S(1)} collective-permute-done((bf16[128,4,512]{2,0,1:T(8,128)(2,1)S(1)}, bf16[128,4,512]{2,0,1:T(8,128)(2,1)S(1)}, u32[]{:S(2)}, u32[]{:S(2)}) %collective-permute-start) | collective-permute-done | bytes 524320 | tf_op jit(solution)/shard_map/ppermute | solution.py:14
  42.5 0.0 copy-start.4
  42.5 0.8 copy-done.4
  43.3 0.0 collective-permute-start.1
  43.3 14.1 %collective-permute-done.1 = bf16[128,4,512]{2,0,1:T(8,128)(2,1)} collective-permute-done((bf16[128,4,512]{2,0,1:T(8,128)(2,1)S(1)}, bf16[128,4,512]{2,0,1:T(8,128)(2,1)}, u32[]{:S(2)}, u32[]{:S(2)}) %collective-permute-start.1) | collective-permute-done | bytes 524320 | tf_op jit(solution)/shard_map/ppermute | solution.py:14
  57.3 0.0 collective-permute-start.2
  57.3 2.3 copy.13
  59.6 1.4 reshape_squeeze.7
  61.1 0.0 copy-done.7
  61.1 0.2 copy.15
  61.3 0.1 reshape.38
  61.4 9.3 %collective-permute-done.2 = bf16[128,4,512]{2,0,1:T(8,128)(2,1)} collective-permute-done((bf16[128,4,512]{2,0,1:T(8,128)(2,1)}, bf16[128,4,512]{2,0,1:T(8,128)(2,1)}, u32[]{:S(2)}, u32[]{:S(2)}) %collective-permute-start.2) | collective-permute-done | bytes 524320 | tf_op jit(solution)/shard_map/ppermute | solution.py:14
  70.7 4.6 %fusion.16 = bf16[512,4,512]{2,0,1:T(8,128)(2,1)S(1)} fusion(s32[]{:T(128)S(6)} %select_n.23, bf16[128,4,512]{2,0,1:T(8,128)(2,1)} %collective-permute-done.2, bf16[128,4,512]{2,0,1:T(8,128)(2,1)} %collective-permute-done.1, bf16[128,4,512]{2,0,1:T(8,128)(2,1)} %copy-done.4, bf16[128,4,512]{2,0,1:T(8,128)(2,1)} %copy-done.2), kind=kLoop, calls=%fused_computation.37 | loop fusion | flops 16777216 | bytes 4194308 | tf_op jit(solution)/shard_map/jit(_roll_dynamic)/concatenate | solution.py:19
  75.2 2.4 copy.12
  77.7 8.1 %fusion = bf16[1536,2048]{0,1:T(8,128)(2,1)} fusion(bf16[512,2048]{0,1:T(8,128)(2,1)} %bitcast.73, bf16[1536,512]{1,0:T(8,128)(2,1)} %reshape_squeeze.7), kind=kOutput, calls=%fused_computation.2 | convolution fusion | flops 3224371200 | bytes 9961472 | tf_op jit(solution)/shard_map/dot_general | solution.py:55
  85.8 8.7 %copy.14 = bf16[1536,2048]{1,0:T(8,128)(2,1)} copy(bf16[1536,2048]{0,1:T(8,128)(2,1)} %fusion) | data formatting | bytes 12582912 | tf_op jit(solution)/shard_map/convert_element_type | solution.py:60
  94.5 10.8 %reshape.37 = bf16[128,48,512]{2,1,0:T(8,128)(2,1)} reshape(bf16[1536,2048]{1,0:T(8,128)(2,1)} %copy.14) | data formatting | bytes 12582912 | tf_op jit(solution)/shard_map/reshape | solution.py:60
  105.2 7.2 %convert_bitcast_fusion.1 = bf16[128,48,512]{2,1,0:T(8,128)(2,1)} fusion(bf16[128,48,512]{2,1,0:T(8,128)(2,1)} %reshape.37, bf16[48,48]{0,1:T(8,128)(2,1)S(1)} %reshape.38), kind=kOutput, calls=%fused_computation.9 | convolution fusion | flops 305135616 | bytes 12587520 | tf_op jit(solution)/shard_map/ik,akb->aib/dot_general | solution.py:63
  112.4 13.6 %reshape.39 = bf16[128,4,6144]{2,1,0:T(4,128)(2,1)} reshape(bf16[128,48,512]{2,1,0:T(8,128)(2,1)} %convert_bitcast_fusion.1) | data formatting | bytes 12582912 | tf_op jit(solution)/shard_map/reshape | solution.py:66
  126.0 0.0 collective-permute-done.3
  126.0 6.1 %broadcast_select_fusion = bf16[1,512,12,512]{1,3,2,0:T(8,128)(2,1)} fusion(bf16[1,512,12,512]{1,3,2,0:T(8,128)(2,1)} %copy.18, bf16[1,512,12,512]{1,3,2,0:T(8,128)(2,1)} %collective-permute-done.3, pred[]{:T(512)S(6)} %eq.5), kind=kLoop, calls=%fused_computation.10 | loop fusion | flops 3145728 | bytes 18874368 | tf_op jit(solution)/shard_map/jit(_where)/select_n | solution.py:43
  132.1 11.5 %fusion.24 = (f32[]{:T(128)}, f32[]{:T(128)}, f32[]{:T(128)}, f32[]{:T(128)}, f32[]{:T(128)}, /*index=5*/f32[128,4,512]{2,0,1:T(8,128)S(1)}) fusion(f32[]{:T(128)S(6)} %sqrt.9, f32[1,128,4,512]{3,2,1,0:T(4,128)S(1)} %copy-done, bf16[512,6144,1]{0,1,2:T(8,128)(2,1)} %bitcast.70, bf16[128,4,6144]{2,1,0:T(4,128)(2,1)} %reshape.39), kind=kOutput, calls=%fused_computation.53 | convolution fusion | flops 3224109056 | bytes 14680088 | tf_op jit(solution)/shard_map/asc,bc->asb/dot_general | solution.py:67
  143.6 9.6 %all-reduce.1 = (f32[]{:T(128)}, f32[]{:T(128)}, f32[]{:T(128)}, f32[]{:T(128)}, f32[]{:T(128)}, /*index=5*/f32[]{:T(128)}) all-reduce(f32[]{:T(128)} %get-tuple-element.19, f32[]{:T(128)} %get-tuple-element.17, f32[]{:T(128)} %get-tuple-element.18, f32[]{:T(128)} %get-tuple-element.16, ...), channel_id=1, replica_groups=mesh['seg'=8,'row'=4] {'row'}, use_global_device_ids=true, to_apply=%region_5.7 | all-reduce | flops 6 | bytes 48 | tf_op jit(solution)/shard_map/psum | solution.py:68
  160.3 1.4 fusion.32
  161.6 0.0 copy-start.3
  161.6 0.8 copy-done.3
  162.5 1.9 collective-permute-start.4
  164.4 10.2 %collective-permute-done.4 = bf16[128,4,512]{2,0,1:T(8,128)(2,1)S(1)} collective-permute-done((bf16[128,4,512]{2,0,1:T(8,128)(2,1)S(1)}, bf16[128,4,512]{2,0,1:T(8,128)(2,1)S(1)}, u32[]{:S(2)}, u32[]{:S(2)}) %collective-permute-start.4) | collective-permute-done | bytes 524320 | tf_op jit(solution)/shard_map/ppermute | solution.py:14
  174.6 0.0 copy-start.5
  174.6 0.8 copy-done.5
  175.4 1.8 collective-permute-start.5
  177.2 12.3 %collective-permute-done.5 = bf16[128,4,512]{2,0,1:T(8,128)(2,1)S(1)} collective-permute-done((bf16[128,4,512]{2,0,1:T(8,128)(2,1)S(1)}, bf16[128,4,512]{2,0,1:T(8,128)(2,1)S(1)}, u32[]{:S(2)}, u32[]{:S(2)}) %collective-permute-start.5) | collective-permute-done | bytes 524320 | tf_op jit(solution)/shard_map/ppermute | solution.py:14
  189.5 0.0 copy-start.6
  189.5 1.5 collective-permute-start.6
  191.7 0.0 copy-done.6
  191.7 8.9 %collective-permute-done.6 = bf16[128,4,512]{2,0,1:T(8,128)(2,1)} collective-permute-done((bf16[128,4,512]{2,0,1:T(8,128)(2,1)S(1)}, bf16[128,4,512]{2,0,1:T(8,128)(2,1)}, u32[]{:S(2)}, u32[]{:S(2)}) %collective-permute-start.6) | collective-permute-done | bytes 524320 | tf_op jit(solution)/shard_map/ppermute | solution.py:14
  200.6 4.6 %fusion.9 = bf16[512,4,512]{2,0,1:T(8,128)(2,1)S(1)} fusion(s32[]{:T(128)S(6)} %select_n.23, bf16[128,4,512]{2,0,1:T(8,128)(2,1)} %collective-permute-done.6, bf16[128,4,512]{2,0,1:T(8,128)(2,1)} %copy-done.6, bf16[128,4,512]{2,0,1:T(8,128)(2,1)} %copy-done.5, bf16[128,4,512]{2,0,1:T(8,128)(2,1)} %copy-done.3), kind=kLoop, calls=%fused_computation.30 | loop fusion | flops 16777216 | bytes 4194308 | tf_op jit(solution)/shard_map/jit(_roll_dynamic)/concatenate | solution.py:19
  205.2 2.4 copy.21
  207.6 8.2 %fusion.1 = bf16[1536,2048]{0,1:T(8,128)(2,1)} fusion(bf16[512,2048]{0,1:T(8,128)(2,1)} %bitcast.72, bf16[1536,512]{1,0:T(8,128)(2,1)} %reshape_squeeze.7), kind=kOutput, calls=%fused_computation.3 | convolution fusion | flops 3224371200 | bytes 9961472 | tf_op jit(solution)/shard_map/dot_general | solution.py:55
  215.7 8.6 %copy.22 = bf16[1536,2048]{1,0:T(8,128)(2,1)} copy(bf16[1536,2048]{0,1:T(8,128)(2,1)} %fusion.1) | data formatting | bytes 12582912 | tf_op jit(solution)/shard_map/convert_element_type | solution.py:60
  224.4 10.7 %reshape.41 = bf16[128,48,512]{2,1,0:T(8,128)(2,1)} reshape(bf16[1536,2048]{1,0:T(8,128)(2,1)} %copy.22) | data formatting | bytes 12582912 | tf_op jit(solution)/shard_map/reshape | solution.py:60
  235.1 7.2 %convert_bitcast_fusion = bf16[128,48,512]{2,1,0:T(8,128)(2,1)} fusion(bf16[128,48,512]{2,1,0:T(8,128)(2,1)} %reshape.41, bf16[48,48]{0,1:T(8,128)(2,1)S(1)} %reshape.38), kind=kOutput, calls=%fused_computation.8 | convolution fusion | flops 305135616 | bytes 12587520 | tf_op jit(solution)/shard_map/ik,akb->aib/dot_general | solution.py:63
  242.3 0.0 copy-start.1
  242.3 13.7 %reshape.42 = bf16[128,4,6144]{2,1,0:T(4,128)(2,1)} reshape(bf16[128,48,512]{2,1,0:T(8,128)(2,1)} %convert_bitcast_fusion) | data formatting | bytes 12582912 | tf_op jit(solution)/shard_map/reshape | solution.py:66
  256.0 0.0 copy-done.1
  256.0 11.7 %fusion.29 = (f32[]{:T(128)}, f32[]{:T(128)}, f32[]{:T(128)}, f32[]{:T(128)}, f32[]{:T(128)}, /*index=5*/f32[128,4,512]{2,0,1:T(8,128)S(1)}) fusion(f32[128,4,512]{2,0,1:T(8,128)S(1)} %copy-done.1, f32[]{:T(128)S(6)} %sqrt.9, f32[1,128,4,512]{3,2,1,0:T(4,128)S(1)} %copy-done, bf16[512,6144,1]{0,1,2:T(8,128)(2,1)} %bitcast.71, bf16[128,4,6144]{2,1,0:T(4,128)(2,1)} %reshape.42), kind=kOutput, calls=%fused_computation.58 | convolution fusion | flops 3224109056 | bytes 15728664 | tf_op jit(solution)/shard_map/asc,bc->asb/dot_general | solution.py:67
  267.7 9.8 %all-reduce = (f32[]{:T(128)}, f32[]{:T(128)}, f32[]{:T(128)}, f32[]{:T(128)}, f32[]{:T(128)}) all-reduce(f32[]{:T(128)} %get-tuple-element.13, f32[]{:T(128)} %get-tuple-element.12, f32[]{:T(128)} %get-tuple-element.11, f32[]{:T(128)} %get-tuple-element.14, f32[]{:T(128)} %get-tuple-element.10), channel_id=1, replica_groups=mesh['seg'=8,'row'=4] {'row'}, use_global_device_ids=true, to_apply=%region_16.18 | all-reduce | flops 5 | bytes 40 | tf_op jit(solution)/shard_map/psum | solution.py:68
  283.4 0.5 fusion.27
  283.9 1.6 copy.26
  285.6 0.6 maximum_bitcast_fusion
Async XLA Ops:
  0.6 10.0 %copy-start = (f32[1,128,4,512]{3,2,1,0:T(4,128)S(1)}, f32[1,128,4,512]{3,2,1,0:T(4,128)}, u32[]{:S(2)}) copy-start(f32[1,128,4,512]{3,2,1,0:T(4,128)} %param.9) | copy-start | bytes 3145732
  9.4 116.7 %collective-permute-start.3 = (bf16[1,512,12,512]{1,3,2,0:T(8,128)(2,1)}, bf16[1,512,12,512]{1,3,2,0:T(8,128)(2,1)}, u32[]{:S(2)}, u32[]{:S(2)}) collective-permute-start(bf16[1,512,12,512]{1,3,2,0:T(8,128)(2,1)} %copy.18), channel_id=1, source_target_pairs={{4,0},{8,4},{12,8},{16,12},{20,16},{24,20},{28,24},{5,1},{9,5},{13... | collective-permute-start | bytes 18874376 | tf_op jit(solution)/shard_map/ppermute | solution.py:30
  26.5 34.6 %copy-start.7 = (bf16[4,12,12,4]{2,3,1,0:T(4,128)(2,1)S(1)}, bf16[4,12,12,4]{2,3,1,0:T(4,128)(2,1)}, u32[]{:S(2)}) copy-start(bf16[4,12,12,4]{2,3,1,0:T(4,128)(2,1)} %param.8) | copy-start | bytes 13828
  26.8 0.8 copy-start.2
  27.6 14.9 %collective-permute-start = (bf16[128,4,512]{2,0,1:T(8,128)(2,1)S(1)}, bf16[128,4,512]{2,0,1:T(8,128)(2,1)S(1)}, u32[]{:S(2)}, u32[]{:S(2)}) collective-permute-start(bf16[128,4,512]{2,0,1:T(8,128)(2,1)S(1)} %bitcast_convert_fusion), channel_id=1, source_target_pairs={{0,1},{1,2},{2,3},{3,0},{4,5},{5,6},{6,7},{7,4},{8,9},{9,10},{10,1... | collective-permute-start | bytes 1572872 | tf_op jit(solution)/shard_map/ppermute | solution.py:14
  42.5 0.8 copy-start.4
  43.3 14.1 %collective-permute-start.1 = (bf16[128,4,512]{2,0,1:T(8,128)(2,1)S(1)}, bf16[128,4,512]{2,0,1:T(8,128)(2,1)}, u32[]{:S(2)}, u32[]{:S(2)}) collective-permute-start(bf16[128,4,512]{2,0,1:T(8,128)(2,1)S(1)} %collective-permute-done), channel_id=1, source_target_pairs={{0,1},{1,2},{2,3},{3,0},{4,5},{5,6},{6,7},{7,4},{8,9},{9,10},{10,1... | collective-permute-start | bytes 1572872 | tf_op jit(solution)/shard_map/ppermute | solution.py:14
  57.3 13.3 %collective-permute-start.2 = (bf16[128,4,512]{2,0,1:T(8,128)(2,1)}, bf16[128,4,512]{2,0,1:T(8,128)(2,1)}, u32[]{:S(2)}, u32[]{:S(2)}) collective-permute-start(bf16[128,4,512]{2,0,1:T(8,128)(2,1)} %collective-permute-done.1), channel_id=1, source_target_pairs={{0,1},{1,2},{2,3},{3,0},{4,5},{5,6},{6,7},{7,4},{8,9},{9,10},{10,1... | collective-permute-start | bytes 1572872 | tf_op jit(solution)/shard_map/ppermute | solution.py:14
  161.6 0.8 copy-start.3
  162.5 12.2 %collective-permute-start.4 = (bf16[128,4,512]{2,0,1:T(8,128)(2,1)S(1)}, bf16[128,4,512]{2,0,1:T(8,128)(2,1)S(1)}, u32[]{:S(2)}, u32[]{:S(2)}) collective-permute-start(bf16[128,4,512]{2,0,1:T(8,128)(2,1)S(1)} %get-tuple-element.31), channel_id=1, source_target_pairs={{0,1},{1,2},{2,3},{3,0},{4,5},{5,6},{6,7},{7,4},{8,9},{9,10},{10,1... | collective-permute-start | bytes 1572872 | tf_op jit(solution)/shard_map/ppermute | solution.py:14
  174.6 0.8 copy-start.5
  175.4 14.1 %collective-permute-start.5 = (bf16[128,4,512]{2,0,1:T(8,128)(2,1)S(1)}, bf16[128,4,512]{2,0,1:T(8,128)(2,1)S(1)}, u32[]{:S(2)}, u32[]{:S(2)}) collective-permute-start(bf16[128,4,512]{2,0,1:T(8,128)(2,1)S(1)} %collective-permute-done.4), channel_id=1, source_target_pairs={{0,1},{1,2},{2,3},{3,0},{4,5},{5,6},{6,7},{7,4},{8,9},{9,10},{10,1... | collective-permute-start | bytes 1572872 | tf_op jit(solution)/shard_map/ppermute | solution.py:14
  189.5 2.2 copy-start.6
  189.5 11.1 %collective-permute-start.6 = (bf16[128,4,512]{2,0,1:T(8,128)(2,1)S(1)}, bf16[128,4,512]{2,0,1:T(8,128)(2,1)}, u32[]{:S(2)}, u32[]{:S(2)}) collective-permute-start(bf16[128,4,512]{2,0,1:T(8,128)(2,1)S(1)} %collective-permute-done.5), channel_id=1, source_target_pairs={{0,1},{1,2},{2,3},{3,0},{4,5},{5,6},{6,7},{7,4},{8,9},{9,10},{10,1... | collective-permute-start | bytes 1572872 | tf_op jit(solution)/shard_map/ppermute | solution.py:14
  242.3 13.7 %copy-start.1 = (f32[128,4,512]{2,0,1:T(8,128)S(1)}, f32[128,4,512]{2,0,1:T(8,128)}, u32[]{:S(2)}) copy-start(f32[128,4,512]{2,0,1:T(8,128)} %get-tuple-element.32) | copy-start | bytes 3145732
